TPU v7x, 32 devices: a whole 2x2x4 slice. The times are simulated.
32 devices in a mesh: row: 4 (over y, x), col: 8 (over z, core).
Axes of the slice: x: 2, y: 2, z: 4, core: 2. Of those that a mesh axis runs over, the one named last changes fastest.
Arguments:
- left_factor: float32 [2048, 512], P(('row', 'col')), may hold values from -0.125 to 0.125
- left_cotangent: float32 [2048, 512], P(('row', 'col')), may hold values from -32 to 32
- right_factor: float32 [6144, 512], P(('col', 'row')), may hold values from -0.078125 to 0.078125
- right_cotangent: float32 [6144, 512], P(('col', 'row')), may hold values from -32 to 32
- singular: float32 [512], replicated, may hold values from 0.5 to 2, as said below
- singular_cotangent: float32 [512], replicated, may hold values from -384 to 384
Outputs:
- matrix_cotangent: float32 [2048, 6144], P('row', 'col')
Inputs may be any that keep to these rules, and one draw needn't show every extreme that they name: `singular`: strictly decreasing; consecutive values differ by at least 0.75 / 512.
All inputs are finite; a program needn't handle non-finite values.
Results may differ from a plain program's by a relative error of at most 0.0003.
Values sent between devices are 32-bit elements; how exact they have to be, the bound alone decides.
A program may use at most 64 MiB of HBM per device.

v0:
```python
import jax
import jax.numpy as jnp
from jax import lax
from jax.sharding import PartitionSpec as P


def linear_core(gram_left, gram_right, singular):
    squares = singular * singular
    spread = squares[None, :] - squares[:, None]
    size_k = singular.shape[0]
    diagonal = jnp.eye(size_k, dtype=jnp.bool_)
    divided = jnp.where(
        diagonal, jnp.float32(0.0), 1.0 / jnp.where(diagonal, jnp.float32(1.0), spread)
    )
    inverse = 1.0 / singular
    core = divided * (gram_left - gram_left.T) * singular[None, :]
    core = core + singular[:, None] * (divided * (gram_right - gram_right.T))
    return core - gram_left * inverse[None, :] - inverse[:, None] * gram_right.T


def local(left_factor, left_cotangent, right_factor, right_cotangent, singular, singular_cotangent):
    highest = lax.Precision.HIGHEST
    dims = (((1,), (1,)), ((), ()))
    inverse = 1.0 / singular
    right_whole, right_cot_whole = (
        lax.all_gather(right_factor, "row", axis=0, tiled=True),
        lax.all_gather(right_cotangent, "row", axis=0, tiled=True),
    )
    scaled_right = right_cot_whole * inverse[None, :]
    local_left = jnp.dot(
        left_factor.T, left_cotangent, precision=highest, preferred_element_type=jnp.float32
    )
    local_right = jnp.dot(
        right_factor.T, right_cotangent, precision=highest, preferred_element_type=jnp.float32
    )
    gram_left, gram_right = lax.psum((local_left, local_right), ("row", "col"))
    core = linear_core(gram_left, gram_right, singular)
    core = core + jnp.diag(singular_cotangent)
    pieces = lax.all_gather((left_factor, left_cotangent), "col", axis=0, tiled=True)
    formed = (
        jnp.dot(pieces[0], core, precision=highest, preferred_element_type=jnp.float32)
        + pieces[1] * inverse[None, :]
    )
    result = lax.dot_general(
        formed, right_whole, dims, precision=highest, preferred_element_type=jnp.float32
    )
    return result + lax.dot_general(
        pieces[0], scaled_right, dims, precision=highest, preferred_element_type=jnp.float32
    )


def solution(mesh):
    placed = (
        P(("row", "col"), None),
        P(("row", "col"), None),
        P(("col", "row"), None),
        P(("col", "row"), None),
        P(),
        P(),
    )
    return jax.shard_map(
        local, mesh=mesh, in_specs=placed, out_specs=P("row", "col"), check_vma=False
    )
```

profile of v0, /device:TPU:0, one launch (start us, length us, event | category | flops | bytes accessed | tf_op | source)
XLA Modules:
  0.0 181.8 jit_solution(15067702836896014263)
XLA Ops:
  7.4 0.0 copy-start.1
  7.4 0.0 copy-start
  7.4 0.0 all-reduce.3.cloned.1.call-start
  7.4 3.1 %fusion.31 = f32[512,512]{1,0:T(8,128)} fusion(f32[64,512]{1,0:T(8,128)} %param.6, f32[64,512]{1,0:T(8,128)} %param.7), kind=kOutput, calls=%fused_computation.36 | convolution fusion | flops 201326592 | bytes 1310720 | tf_op jit(solution)/shard_map/dot_general | solution.py:30
  10.5 0.0 copy-done.1
  10.5 0.0 copy-done
  10.5 2.1 %fusion.32 = f32[512,512]{0,1:T(8,128)} fusion(f32[192,512]{1,0:T(8,128)S(1)} %copy-done.1, f32[192,512]{1,0:T(8,128)S(1)} %copy-done), kind=kOutput, calls=%fused_computation.37 | convolution fusion | flops 603979776 | bytes 1835008 | tf_op jit(solution)/shard_map/dot_general | solution.py:33
  12.6 0.0 copy-start.5
  12.6 0.0 all-reduce.3.cloned.1.call-update
  12.6 0.0 all-gather.5.cloned.1.call-start
  12.7 0.5 all-gather.5.cloned.1.call-update
  13.2 0.0 all-gather.7.cloned.1.call-start
  13.2 0.5 all-gather.7.cloned.1.call-update
  13.8 0.0 all-gather.11.cloned.1.call-start
  13.8 0.5 all-gather.11.cloned.1.call-update
  14.3 0.0 all-gather.9.cloned.1.call-start
  14.4 0.7 all-gather.9.cloned.1.call-update
  15.1 0.0 copy-done.5
  15.1 141.0 %all-reduce.3.cloned.1.call-done = (f32[512,512]{0,1:T(8,128)}, f32[512,512]{1,0:T(8,128)}) async-done(((f32[512,512]{0,1:T(8,128)}, f32[512,512]{1,0:T(8,128)}), (f32[512,512]{0,1:T(8,128)}, f32[512,512]{1,0:T(8,128)})) %all-reduce.3.cloned.1.call-update) | async-done | bytes 2097168 | tf_op jit(solution)/shard_map/psum | solution.py:36
  156.1 0.0 copy-start.2
  156.1 1.6 copy.7
  157.7 0.0 copy-start.3
  157.7 0.0 copy-start.6
  157.7 0.0 copy-done.2
  157.8 1.3 copy.9
  159.1 0.0 all-gather.5.cloned.1.call-done
  159.1 0.0 all-gather.7.cloned.1.call-done
  159.1 0.0 copy-done.3
  159.1 0.0 copy-done.6
  159.1 5.3 %fusion.2 = f32[512,512]{1,0:T(8,128)} fusion(f32[512,512]{1,0:T(8,128)} %all-gather.5.cloned.1.call-done, f32[512,512]{1,0:T(8,128)} %copy.9, f32[512,512]{0,1:T(8,128)S(1)} %copy-done.2, f32[512,512]{1,0:T(8,128)S(1)} %copy-done.3, f32[512,512]{0,1:T(8,128)S(1)} %copy.7, f32[512,512]{1,0:T(8,128)} %all-gather.7.cloned.1.call-done, f32[512]{0:T(512)S(1)} %copy-done.6, ...), kind=kOutput, calls=%fused_computation.4 | convolution fusion | flops 1615855616 | bytes 7348224 | tf_op jit(solution)/shard_map/dot_general | solution.py:41
  164.4 0.0 copy-start.4
  164.4 0.0 all-gather.11.cloned.1.call-done
  164.4 4.5 %fusion = f32[768,512]{0,1:T(8,128)S(1)} fusion(f32[512,512]{1,0:T(8,128)} %all-gather.5.cloned.1.call-done, f32[768,512]{1,0:T(8,128)} %all-gather.11.cloned.1.call-done, f32[512]{0:T(512)S(1)} %get-tuple-element.7), kind=kOutput, calls=%fused_computation.1 | convolution fusion | flops 2416312320 | bytes 4196352 | tf_op jit(solution)/shard_map/dot_general | solution.py:47
  168.9 0.0 all-gather.9.cloned.1.call-done
  168.9 0.0 copy-done.4
  168.9 5.3 %bitcast_add_fusion = f32[512,768]{1,0:T(8,128)} fusion(f32[768,512]{0,1:T(8,128)S(1)} %fusion, f32[512,512]{1,0:T(8,128)S(1)} %copy-done.4, f32[768,512]{1,0:T(8,128)} %all-gather.9.cloned.1.call-done), kind=kOutput, calls=%fused_computation | convolution fusion | flops 2416312320 | bytes 5767168 | tf_op jit(solution)/shard_map/dot_general | solution.py:44
  (1 shorter events, 0.0 us)
Async XLA Ops:
  7.4 3.1 %copy-start.1 = (f32[192,512]{1,0:T(8,128)S(1)}, f32[192,512]{1,0:T(8,128)}, u32[]{:S(2)}) copy-start(f32[192,512]{1,0:T(8,128)} %param.8) | copy-start | bytes 1179652
  7.4 3.1 %copy-start = (f32[192,512]{1,0:T(8,128)S(1)}, f32[192,512]{1,0:T(8,128)}, u32[]{:S(2)}) copy-start(f32[192,512]{1,0:T(8,128)} %param.9) | copy-start | bytes 1179652
  7.4 148.7 %all-reduce.3.cloned.1.call-start = ((), (), s32[]{:S(2)}) async-start(), calls=%async_computation.4 | async-start | bytes 4194304 | tf_op jit(solution)/shard_map/psum | solution.py:36
  12.6 2.5 %copy-start.5 = (f32[512]{0:T(512)S(1)}, f32[512]{0:T(512)}, u32[]{:S(2)}) copy-start(f32[512]{0:T(512)} %param.10) | copy-start | bytes 6148
  12.6 146.5 %all-gather.5.cloned.1.call-start = ((), (), s32[]{:S(2)}) async-start(), calls=%async_computation | async-start | bytes 1179648 | tf_op jit(solution)/shard_map/all_gather | solution.py:39
  13.2 145.9 %all-gather.7.cloned.1.call-start = ((), (), s32[]{:S(2)}) async-start(), calls=%async_computation.1 | async-start | bytes 1179648 | tf_op jit(solution)/shard_map/all_gather | solution.py:39
  13.8 150.6 %all-gather.11.cloned.1.call-start = ((), (), s32[]{:S(2)}) async-start(), calls=%async_computation.3 | async-start | bytes 1966080 | tf_op jit(solution)/shard_map/all_gather | solution.py:27
  14.3 154.6 %all-gather.9.cloned.1.call-start = ((), (), s32[]{:S(2)}) async-start(), calls=%async_computation.2 | async-start | bytes 1966080 | tf_op jit(solution)/shard_map/all_gather | solution.py:26
  156.1 1.7 copy-start.2
  157.7 1.3 copy-start.3
  157.7 1.3 copy-start.6
  164.4 4.6 %copy-start.4 = (f32[512,512]{1,0:T(8,128)S(1)}, f32[512,512]{1,0:T(8,128)}, u32[]{:S(2)}) copy-start(f32[512,512]{1,0:T(8,128)} %fusion.2) | copy-start | bytes 3145732
Sparse Core Ops, SparseCore 0:
  13.7 142.3 all-reduce.2
Sparse Core Ops, SparseCore 1:
  14.7 26.9 all-gather.4
  43.1 22.2 all-gather.6
  67.1 30.5 all-gather.10
  99.6 31.0 all-gather.8
where the time goes:
time: 182 us
  waiting for transfers between devices  143 us (79%)
  matrix products  20.3 us (11%)
  between operations  15.1 us (8%)
  local copies, waits for them, and re-layouts  2.98 us (2%)
    psum x1, waiting for transfers between devices, local(): gram_left, gram_right = lax.psum((local_left, local_right), ('row', 'col'))  141 us
    dot_general x1, matrix products, local(): jnp.dot(pieces[0], core, precision=highest, preferred_element_type=jnp.fl...  5.3 us
    dot_general x1, matrix products, local(): lax.dot_general(formed, right_whole, dims, precision=highest, preferred_e...  5.29 us
    dot_general x1, matrix products, local(): lax.dot_general(pieces[0], scaled_right, dims, precision=highest, preferr...  4.51 us
  transfers between devices with their start and end apart: 5, of which 1 were waited for; matrix products, arithmetic and copies ran while one was open for 7% of the time, Pallas kernels for 0%

commit v1 on v0

v1 whole, which is shorter than its diff:
```python
import functools
import math

import jax
import jax.numpy as jnp
from jax import lax
from jax.experimental import pallas as pl
from jax.experimental.pallas import tpu as pltpu
from jax.sharding import PartitionSpec as P

MESH = pl.DeviceIdType.MESH
F32 = jnp.float32
BF16 = jnp.bfloat16
LANES = 128
NT = (((1,), (1,)), ((), ()))
NN = (((1,), (0,)), ((), ()))
TN = (((0,), (0,)), ((), ()))


def split(x):
    hi = x.astype(BF16)
    return hi, (x - hi.astype(F32)).astype(BF16)


def dot3(ah, al, bh, bl, dims):
    dot = functools.partial(lax.dot_general, dimension_numbers=dims, preferred_element_type=F32)
    return dot(ah, bh) + (dot(ah, bl) + dot(al, bh))


def kernel(
    R, C,
    u_ref, uc_ref, v_ref, vc_ref, s_ref, sc_ref, out_ref,
    ug, ucg, vg, vcg, gl, gr, scol, part, ra, p1, rb, rc, core,
    wh, wl, uh, ul, lh, ll, xh, xl,
    send_v, send_u, send_r, send_c, recv_v, recv_u, recv_a, recv_b, recv_c, recv_d, recv_e,
):
    n = math.isqrt(R)
    Z = C // 2
    r, c = lax.axis_index("row"), lax.axis_index("col")
    a, b = r // n, r % n
    z, h = c // 2, c % 2
    sib = (r, c + 1 - 2 * h)
    um, vm = u_ref.shape[0], v_ref.shape[0]
    K = u_ref.shape[1]
    half = K // 2
    blk = half // R

    def row_peer(k):
        return lax.rem(r + k, R)

    def z_peer(k):
        return lax.rem(z + k, Z)

    def a_peer(k):
        return lax.rem(a + k, n)

    def b_peer(k):
        return lax.rem(b + k, n)

    barrier = pltpu.get_barrier_semaphore()
    pl.semaphore_signal(barrier, inc=1, device_id=sib, device_id_type=MESH)
    for k in range(1, R):
        pl.semaphore_signal(barrier, inc=1, device_id=(row_peer(k), c), device_id_type=MESH)
    for k in range(1, Z):
        pl.semaphore_signal(barrier, inc=1, device_id=(r, 2 * z_peer(k) + h), device_id_type=MESH)
    pl.semaphore_wait(barrier, 1 + (R - 1) + (Z - 1))

    sends = []
    counts = {"v": 0, "u": 0, "r": 0, "c": 0}
    pools = {"v": send_v, "u": send_u, "r": send_r, "c": send_c}

    def push(pool, src, dst, recv, to):
        i = counts[pool]
        counts[pool] = i + 1
        copy = pltpu.make_async_remote_copy(
            src_ref=src, dst_ref=dst, send_sem=pools[pool].at[i], recv_sem=recv,
            device_id=to, device_id_type=MESH,
        )
        copy.start()
        sends.append(copy)

    def await_recv(dst, recv):
        pltpu.make_async_remote_copy(
            src_ref=dst, dst_ref=dst, send_sem=send_v.at[0], recv_sem=recv,
            device_id=sib, device_id_type=MESH,
        ).wait_recv()

    def rows(ref, index, size):
        return ref.at[pl.ds(pl.multiple_of(index * size, size), size)]

    vbuf, ubuf = (vg, vcg), (ug, ucg)
    vsrc, usrc = (v_ref, vc_ref), (u_ref, uc_ref)

    for k in range(1, n):
        push("v", v_ref, rows(vg, r, vm), recv_v.at[0, r], (a * n + b_peer(k), c))
    for k in range(1, n):
        push("v", vc_ref, rows(vcg, r, vm), recv_v.at[1, r], (a_peer(k) * n + b, c))
    for t in range(2):
        for k in range(1, Z):
            push("u", usrc[t], rows(ubuf[t], c, um), recv_u.at[t, c], (r, 2 * z_peer(k) + h))
    for k in range(1, n):
        push("v", v_ref, rows(vg, r, vm), recv_v.at[0, r], (a_peer(k) * n + b, c))
    for k in range(1, n):
        push("v", vc_ref, rows(vcg, r, vm), recv_v.at[1, r], (a * n + b_peer(k), c))
    for t in range(2):
        push("c", usrc[t], rows(ubuf[t], c, um), recv_u.at[t, c], sib)

    highest = lax.Precision.HIGHEST
    gl[...] = lax.dot_general(u_ref[...], uc_ref[...], TN, precision=highest, preferred_element_type=F32)
    gr[...] = lax.dot_general(v_ref[...], vc_ref[...], TN, precision=highest, preferred_element_type=F32)
    s_row = s_ref[...]
    inv_row = 1.0 / s_row
    scol[...] = jnp.broadcast_to(s_row, (LANES, K)).T

    @pl.loop(0, K // LANES)
    def _(i):
        here = pl.ds(pl.multiple_of(i * LANES, LANES), LANES)
        s_col = scol[here, 0:1]
        inv_col = 1.0 / s_col
        spread = s_row * s_row - s_col * s_col
        row_id = i * LANES + lax.broadcasted_iota(jnp.int32, (LANES, K), 0)
        diagonal = row_id == lax.broadcasted_iota(jnp.int32, (LANES, K), 1)
        divided = jnp.where(diagonal, 0.0, 1.0 / jnp.where(diagonal, 1.0, spread))
        left, left_t = gl[here, :], gl[:, here].T
        right, right_t = gr[here, :], gr[:, here].T
        value = divided * (left - left_t) * s_row + s_col * (divided * (right - right_t))
        part[here, :] = value - left * inv_row - inv_col * right_t

    push("c", rows(part, 1 - h, half), ra, recv_a.at[0], sib)
    rows(ug, c, um)[...] = u_ref[...]
    rows(ucg, c, um)[...] = uc_ref[...]
    rows(vg, r, vm)[...] = v_ref[...]
    rows(vcg, r, vm)[...] = vc_ref[...]
    await_recv(ra, recv_a.at[0])
    p1[...] = rows(part, h, half)[...] + ra[...]
    for k in range(1, R):
        push("r", rows(p1, row_peer(k), blk), rows(rb, r, blk), recv_b.at[r], (row_peer(k), c))
    rows(rb, r, blk)[...] = rows(p1, r, blk)[...]
    for k in range(1, R):
        await_recv(rows(rb, row_peer(k), blk), recv_b.at[row_peer(k)])
    total = rb[0:blk, :]
    for q in range(1, R):
        total = total + rb[q * blk:(q + 1) * blk, :]
    rows(rc, z, blk)[...] = total
    for k in range(1, Z):
        push("r", rows(rc, z, blk), rows(rc, z, blk), recv_c.at[z], (r, 2 * z_peer(k) + h))

    for k in range(1, n):
        src = a * n + b_peer(k)
        await_recv(rows(vg, src, vm), recv_v.at[0, src])
        for j in range(1, n):
            push("v", rows(vg, src, vm), rows(vg, src, vm), recv_v.at[0, src], (a_peer(j) * n + b, c))
    for k in range(1, n):
        src = a_peer(k) * n + b
        await_recv(rows(vcg, src, vm), recv_v.at[1, src])
        for j in range(1, n):
            push("v", rows(vcg, src, vm), rows(vcg, src, vm), recv_v.at[1, src], (a * n + b_peer(j), c))

    for k in range(1, Z):
        await_recv(rows(rc, z_peer(k), blk), recv_c.at[z_peer(k)])
    total = rc[0:blk, :]
    for q in range(1, Z):
        total = total + rc[q * blk:(q + 1) * blk, :]
    mine = h * R + r
    row_id = mine * blk + lax.broadcasted_iota(jnp.int32, (blk, K), 0)
    diagonal = row_id == lax.broadcasted_iota(jnp.int32, (blk, K), 1)
    rows(core, mine, blk)[...] = total + jnp.where(diagonal, sc_ref[...], 0.0)
    for k in range(1, R):
        push("r", rows(core, mine, blk), rows(core, mine, blk), recv_d.at[r], (row_peer(k), c))
    push("c", rows(core, mine, blk), rows(core, mine, blk), recv_e.at[r], sib)

    for k in range(1, Z):
        src = 2 * z_peer(k) + h
        for t in range(2):
            await_recv(rows(ubuf[t], src, um), recv_u.at[t, src])
            push("c", rows(ubuf[t], src, um), rows(ubuf[t], src, um), recv_u.at[t, src], sib)

    for k in range(1, R):
        q = row_peer(k)
        await_recv(rows(core, h * R + q, blk), recv_d.at[q])
        push("c", rows(core, h * R + q, blk), rows(core, h * R + q, blk), recv_e.at[q], sib)
    for k in range(Z):
        src = 2 * z_peer(k) + 1 - h
        for t in range(2):
            await_recv(rows(ubuf[t], src, um), recv_u.at[t, src])

    uh[...], ul[...] = split(ug[...])
    xh[...], xl[...] = split(ug[...] * inv_row)
    late_a, late_b = [], []
    for k in range(1, n):
        await_recv(rows(vcg, a * n + b_peer(k), vm), recv_v.at[1, a * n + b_peer(k)])
        await_recv(rows(vg, a_peer(k) * n + b, vm), recv_v.at[0, a_peer(k) * n + b])
    for k in range(1, n):
        for j in range(1, n):
            src = a_peer(k) * n + b_peer(j)
            await_recv(rows(vcg, src, vm), recv_v.at[1, src])
            await_recv(rows(vg, src, vm), recv_v.at[0, src])
    width = 2 * LANES

    @pl.loop(0, out_ref.shape[1] // width)
    def _(i):
        here = pl.ds(pl.multiple_of(i * width, width), width)
        bh, bl = split(vcg[here, :])
        out_ref[:, here] = dot3(xh[...], xl[...], bh, bl, NT)

    for q in range(R):
        at = (1 - h) * R + q
        await_recv(rows(core, at, blk), recv_e.at[q])
    wh[...], wl[...] = split(core[...])

    @pl.loop(0, K // width)
    def _(i):
        here = pl.ds(pl.multiple_of(i * width, width), width)
        panel = dot3(uh[...], ul[...], wh[:, here], wl[:, here], NN)
        panel = panel + ucg[:, here] * (1.0 / s_ref[:, here])
        lh[:, here], ll[:, here] = split(panel)

    @pl.loop(0, out_ref.shape[1] // width)
    def _(i):
        here = pl.ds(pl.multiple_of(i * width, width), width)
        bh, bl = split(vg[here, :])
        out_ref[:, here] += dot3(lh[...], ll[...], bh, bl, NT)

    for copy in sends:
        copy.wait_send()


def local(R, C, left_factor, left_cotangent, right_factor, right_cotangent, singular, singular_cotangent):
    um, K = left_factor.shape
    vm = right_factor.shape[0]
    n, Z = math.isqrt(R), C // 2
    M, N = um * C, vm * R
    blk = K // 2 // R
    vmem = pl.BlockSpec(memory_space=pltpu.VMEM)
    dma = pltpu.SemaphoreType.DMA
    f32 = [
        (M, K), (M, K), (N, K), (N, K), (K, K), (K, K), (K, LANES), (K, K),
        (K // 2, K), (K // 2, K), (R * blk, K), (Z * blk, K), (K, K),
    ]
    b16 = [(K, K)] * 2 + [(M, K)] * 6
    scratch = [pltpu.VMEM(shape, F32) for shape in f32] + [pltpu.VMEM(shape, BF16) for shape in b16]
    scratch += [
        dma((4 * (n - 1) + 2 * (n - 1) ** 2,)), dma((2 * (Z - 1),)),
        dma((2 * (R - 1) + Z - 1,)), dma((2 + 1 + 1 + 2 * (Z - 1) + R - 1,)),
        dma((2, R)), dma((2, C)), dma((1,)), dma((R,)), dma((Z,)), dma((R,)), dma((R,)),
    ]
    return pl.pallas_call(
        functools.partial(kernel, R, C),
        out_shape=jax.ShapeDtypeStruct((M, N), F32),
        in_specs=[vmem] * 6,
        out_specs=vmem,
        scratch_shapes=scratch,
        compiler_params=pltpu.CompilerParams(
            collective_id=0, has_side_effects=True, vmem_limit_bytes=48 * 1024 * 1024
        ),
    )(
        left_factor, left_cotangent, right_factor, right_cotangent,
        singular.reshape(1, K), singular_cotangent.reshape(1, K),
    )


def solution(mesh):
    placed = (
        P(("row", "col"), None),
        P(("row", "col"), None),
        P(("col", "row"), None),
        P(("col", "row"), None),
        P(),
        P(),
    )
    return jax.shard_map(
        functools.partial(local, mesh.shape["row"], mesh.shape["col"]),
        mesh=mesh, in_specs=placed, out_specs=P("row", "col"), check_vma=False,
    )
```

time: 182 us -> 58.4 us (0.32)
  waiting for transfers between devices: 143 us -> 0 us
  Pallas kernels: 0 us -> 51.6 us
  matrix products: 20.3 us -> 0 us
  between operations: 15.1 us -> 0.02 us
  local copies, waits for them, and re-layouts: 2.98 us -> 6.31 us
    psum x1 -> x0, waiting for transfers between devices: 141 us -> none  [local(): gram_left, gram_right = lax.psum((local_left, local_right), ('row', 'col'))]
    pallas_call x0 -> x1, Pallas kernels: none -> 51.6 us  [local(): pl.pallas_call(functools.partial(kernel, R, C), out_shape=jax.ShapeDtypeS...]
    dot_general x5 -> x0, matrix products: 20.3 us -> none  [the longest x1 5.3 us: local(): jnp.dot(pieces[0], core, precision=highest, preferred_element_type=jnp.fl...]
    unnamed x14 -> x13, local copies, waits for them, and re-layouts: 0.03 us -> 6.31 us
    psum x2 -> x0, local copies, waits for them, and re-layouts: 2.95 us -> none  [local(): gram_left, gram_right = lax.psum((local_left, local_right), ('row', 'col'))]
    unnamed x5 -> x0, waiting for transfers between devices: 2.27 us -> none
  transfers between devices with their start and end apart: 5 -> 0, of which waited for: 1 -> 0; matrix products, arithmetic and copies ran while one was open for 7% -> 0% of each run, Pallas kernels for 0% -> 0%
where the time goes in v1:
time: 58.4 us; the launch traced here: 57.9 us
  Pallas kernels  51.6 us (88%)
  local copies, waits for them, and re-layouts  6.31 us (11%)
    pallas_call x1, Pallas kernels, local(): pl.pallas_call(functools.partial(kernel, R, C), out_shape=jax.ShapeDtypeS...  51.6 us
    unnamed x13, local copies, waits for them, and re-layouts  6.31 us

profile of v1, /device:TPU:0, one launch (start us, length us, event | category | flops | bytes accessed | tf_op | source)
XLA Modules:
  0.0 57.9 jit_solution(9291101013329751414)
XLA Ops:
  0.0 0.0 copy-start
  0.0 1.0 %copy-done = f32[192,512]{1,0:T(8,128)S(1)} copy-done((f32[192,512]{1,0:T(8,128)S(1)}, f32[192,512]{1,0:T(8,128)}, u32[]{:S(2)}) %copy-start) | copy-done | bytes 393240
  1.0 0.0 copy-start.1
  1.0 1.0 %copy-done.1 = f32[192,512]{1,0:T(8,128)S(1)} copy-done((f32[192,512]{1,0:T(8,128)S(1)}, f32[192,512]{1,0:T(8,128)}, u32[]{:S(2)}) %copy-start.1) | copy-done | bytes 393240
  2.0 0.0 copy-start.2
  2.0 0.9 %copy-done.2 = f32[64,512]{1,0:T(8,128)S(1)} copy-done((f32[64,512]{1,0:T(8,128)S(1)}, f32[64,512]{1,0:T(8,128)}, u32[]{:S(2)}) %copy-start.2) | copy-done | bytes 131096
  2.9 0.0 copy-start.3
  2.9 0.9 %copy-done.3 = f32[64,512]{1,0:T(8,128)S(1)} copy-done((f32[64,512]{1,0:T(8,128)S(1)}, f32[64,512]{1,0:T(8,128)}, u32[]{:S(2)}) %copy-start.3) | copy-done | bytes 131096
  3.8 0.0 copy-start.4
  3.8 0.7 %copy-done.4 = f32[512]{0:T(512)S(1)} copy-done((f32[512]{0:T(512)S(1)}, f32[512]{0:T(512)}, u32[]{:S(2)}) %copy-start.4) | copy-done | bytes 2072
  4.5 0.0 copy-start.5
  4.5 0.7 %copy-done.5 = f32[512]{0:T(512)S(1)} copy-done((f32[512]{0:T(512)S(1)}, f32[512]{0:T(512)}, u32[]{:S(2)}) %copy-start.5) | copy-done | bytes 2072
  5.2 51.6 %shard_map.64 = f32[512,768]{1,0:T(8,128)S(1)} custom-call(f32[64,512]{1,0:T(8,128)S(1)} %copy-done.2, f32[64,512]{1,0:T(8,128)S(1)} %copy-done.3, f32[192,512]{1,0:T(8,128)S(1)} %copy-done, f32[192,512]{1,0:T(8,128)S(1)} %copy-done.1, f32[1,512]{1,0:T(1,128)S(1)} %bitcast.2, f32[1,512]{1,0:T(1,128)S(1)} %bitcast.3), custom_call_target="tpu_custom_call" | custom-call | tf_op jit(solution)/shard_map/pallas_call | solution.py:247
  56.8 1.1 %copy.8 = f32[512,768]{1,0:T(8,128)} copy(f32[512,768]{1,0:T(8,128)S(1)} %shard_map.64) | data formatting | bytes 3145728
Async XLA Ops:
  0.0 1.0 %copy-start = (f32[192,512]{1,0:T(8,128)S(1)}, f32[192,512]{1,0:T(8,128)}, u32[]{:S(2)}) copy-start(f32[192,512]{1,0:T(8,128)} %v_ref.1) | copy-start | bytes 1179652
  1.0 1.0 %copy-start.1 = (f32[192,512]{1,0:T(8,128)S(1)}, f32[192,512]{1,0:T(8,128)}, u32[]{:S(2)}) copy-start(f32[192,512]{1,0:T(8,128)} %vc_ref.1) | copy-start | bytes 1179652
  2.0 0.9 %copy-start.2 = (f32[64,512]{1,0:T(8,128)S(1)}, f32[64,512]{1,0:T(8,128)}, u32[]{:S(2)}) copy-start(f32[64,512]{1,0:T(8,128)} %u_ref.1) | copy-start | bytes 393220
  2.9 0.9 %copy-start.3 = (f32[64,512]{1,0:T(8,128)S(1)}, f32[64,512]{1,0:T(8,128)}, u32[]{:S(2)}) copy-start(f32[64,512]{1,0:T(8,128)} %uc_ref.1) | copy-start | bytes 393220
  3.8 0.7 %copy-start.4 = (f32[512]{0:T(512)S(1)}, f32[512]{0:T(512)}, u32[]{:S(2)}) copy-start(f32[512]{0:T(512)} %param.10) | copy-start | bytes 6148
  4.5 0.7 %copy-start.5 = (f32[512]{0:T(512)S(1)}, f32[512]{0:T(512)}, u32[]{:S(2)}) copy-start(f32[512]{0:T(512)} %param.11) | copy-start | bytes 6148

commit v2 on v1

v2 whole, which is shorter than its diff:
```python
import functools
import math

import jax
import jax.numpy as jnp
from jax import lax
from jax.experimental import pallas as pl
from jax.experimental.pallas import tpu as pltpu
from jax.sharding import PartitionSpec as P

MESH = pl.DeviceIdType.MESH
F32 = jnp.float32
BF16 = jnp.bfloat16
LANES = 128
NT = (((1,), (1,)), ((), ()))
NN = (((1,), (0,)), ((), ()))
TN = (((0,), (0,)), ((), ()))


def split(x):
    hi = x.astype(BF16)
    return hi, (x - hi.astype(F32)).astype(BF16)


def dot3(ah, al, bh, bl, dims):
    dot = functools.partial(lax.dot_general, dimension_numbers=dims, preferred_element_type=F32)
    return dot(ah, bh) + (dot(ah, bl) + dot(al, bh))


def kernel(
    R, C,
    u_ref, uc_ref, v_ref, vc_ref, s_ref, sc_ref, out_ref,
    ug, ucg, vg, vcg, gl, gr, scol, part, ra, p1, rb, p2, rc, core,
    wh, wl, uh, ul, lh, ll, xh, xl,
    load, send, recv_v, recv_u, recv_a, recv_b, recv_c, recv_d, recv_e, recv_f,
):
    n = math.isqrt(R)
    Z = C // 2
    r, c = lax.axis_index("row"), lax.axis_index("col")
    a, b = r // n, r % n
    z, h = c // 2, c % 2
    sib = (r, c + 1 - 2 * h)
    um, vm = u_ref.shape[0], v_ref.shape[0]
    K = u_ref.shape[1]
    half = K // 2
    blk = half // R
    piece = blk // Z if blk % (8 * Z) == 0 else blk

    def row_peer(k):
        return lax.rem(r + k, R)

    def z_peer(k):
        return lax.rem(z + k, Z)

    def a_peer(k):
        return lax.rem(a + k, n)

    def b_peer(k):
        return lax.rem(b + k, n)

    def rows(ref, index, size):
        return ref.at[pl.ds(pl.multiple_of(index * size, size), size)]

    loads = [
        pltpu.make_async_copy(src, dst, load.at[i])
        for i, (src, dst) in enumerate((
            (u_ref, rows(ug, c, um)), (uc_ref, rows(ucg, c, um)),
            (v_ref, rows(vg, r, vm)), (vc_ref, rows(vcg, r, vm)),
        ))
    ]
    for copy in loads:
        copy.start()

    barrier = pltpu.get_barrier_semaphore()
    pl.semaphore_signal(barrier, inc=1, device_id=sib, device_id_type=MESH)
    for k in range(1, R):
        pl.semaphore_signal(barrier, inc=1, device_id=(row_peer(k), c), device_id_type=MESH)
    for k in range(1, Z):
        pl.semaphore_signal(barrier, inc=1, device_id=(r, 2 * z_peer(k) + h), device_id_type=MESH)
    pl.semaphore_wait(barrier, 1 + (R - 1) + (Z - 1))

    sends = []

    def push(tag, src, dst, recv, to):
        copy = pltpu.make_async_remote_copy(
            src_ref=src, dst_ref=dst, send_sem=send.at[len(sends)], recv_sem=recv,
            device_id=to, device_id_type=MESH,
        )
        copy.start()
        sends.append(copy)

    def await_recv(tag, dst, recv):
        pltpu.make_async_remote_copy(
            src_ref=dst, dst_ref=dst, send_sem=send.at[0], recv_sem=recv,
            device_id=sib, device_id_type=MESH,
        ).wait_recv()


    for k in range(1, n):
        push("v", v_ref, rows(vg, r, vm), recv_v.at[0, r], (a * n + b_peer(k), c))
    for k in range(1, n):
        push("v", vc_ref, rows(vcg, r, vm), recv_v.at[1, r], (a_peer(k) * n + b, c))
    for k in range(1, Z):
        push("u", u_ref, rows(ug, c, um), recv_u.at[0, c], (r, 2 * z_peer(k) + h))

    highest = lax.Precision.HIGHEST
    for copy in loads:
        copy.wait()
    gl[...] = lax.dot_general(
        rows(ug, c, um)[...], rows(ucg, c, um)[...], TN, precision=highest, preferred_element_type=F32
    )
    gr[...] = lax.dot_general(
        rows(vg, r, vm)[...], rows(vcg, r, vm)[...], TN, precision=highest, preferred_element_type=F32
    )
    s_row = s_ref[...]
    inv_row = 1.0 / s_row
    scol[...] = jnp.broadcast_to(s_row, (LANES, K)).T

    @pl.loop(0, K // LANES)
    def _(i):
        here = pl.ds(pl.multiple_of(i * LANES, LANES), LANES)
        s_col = scol[here, 0:1]
        inv_col = 1.0 / s_col
        spread = s_row * s_row - s_col * s_col
        row_id = i * LANES + lax.broadcasted_iota(jnp.int32, (LANES, K), 0)
        diagonal = row_id == lax.broadcasted_iota(jnp.int32, (LANES, K), 1)
        divided = jnp.where(diagonal, 0.0, 1.0 / jnp.where(diagonal, 1.0, spread))
        left, left_t = gl[here, :], gl[:, here].T
        right, right_t = gr[here, :], gr[:, here].T
        value = divided * (left - left_t) * s_row + s_col * (divided * (right - right_t))
        part[here, :] = value - left * inv_row - inv_col * right_t

    push("a", rows(part, 1 - h, half), ra, recv_a.at[0], sib)
    await_recv("a", ra, recv_a.at[0])
    p1[...] = rows(part, h, half)[...] + ra[...]
    for k in range(1, R):
        push("b", rows(p1, row_peer(k), blk), rows(rb, r, blk), recv_b.at[r], (row_peer(k), c))
    rows(rb, r, blk)[...] = rows(p1, r, blk)[...]
    for k in range(1, n):
        push("v", v_ref, rows(vg, r, vm), recv_v.at[0, r], (a_peer(k) * n + b, c))
    for k in range(1, n):
        push("v", vc_ref, rows(vcg, r, vm), recv_v.at[1, r], (a * n + b_peer(k), c))
    push("w", u_ref, rows(ug, c, um), recv_u.at[0, c], sib)
    push("w", uc_ref, rows(ucg, c, um), recv_u.at[1, c], sib)
    for k in range(1, R):
        await_recv("b", rows(rb, row_peer(k), blk), recv_b.at[row_peer(k)])
    total = rb[0:blk, :]
    for q in range(1, R):
        total = total + rb[q * blk:(q + 1) * blk, :]

    def stage_2():
        for k in range(1, n):
            src = a * n + b_peer(k)
            await_recv("v", rows(vg, src, vm), recv_v.at[0, src])
            for j in range(1, n):
                push("v", rows(vg, src, vm), rows(vg, src, vm), recv_v.at[0, src], (a_peer(j) * n + b, c))
        for k in range(1, n):
            src = a_peer(k) * n + b
            await_recv("v", rows(vcg, src, vm), recv_v.at[1, src])
            for j in range(1, n):
                push("v", rows(vcg, src, vm), rows(vcg, src, vm), recv_v.at[1, src], (a * n + b_peer(j), c))

    def left_cotangents():
        for k in range(1, Z):
            push("u", uc_ref, rows(ucg, c, um), recv_u.at[1, c], (r, 2 * z_peer(k) + h))

    mine = h * R + r
    if piece != blk:
        p2[...] = total
        for k in range(1, Z):
            push("c", rows(p2, z_peer(k), piece), rows(rc, z, piece), recv_c.at[z], (r, 2 * z_peer(k) + h))
        rows(rc, z, piece)[...] = rows(p2, z, piece)[...]
    else:
        rows(rc, z, blk)[...] = total
        for k in range(1, Z):
            push("c", rows(rc, z, blk), rows(rc, z, blk), recv_c.at[z], (r, 2 * z_peer(k) + h))
    for k in range(1, Z):
        await_recv("c", rows(rc, z_peer(k), piece), recv_c.at[z_peer(k)])
    total = rc[0:piece, :]
    for q in range(1, Z):
        total = total + rc[q * piece:(q + 1) * piece, :]
    at = mine * (blk // piece) + (z if piece != blk else 0)
    row_id = at * piece + lax.broadcasted_iota(jnp.int32, (piece, K), 0)
    diagonal = row_id == lax.broadcasted_iota(jnp.int32, (piece, K), 1)
    rows(core, at, piece)[...] = total + jnp.where(diagonal, sc_ref[...], 0.0)
    if piece != blk:
        for k in range(1, Z):
            push("f", rows(core, at, piece), rows(core, at, piece), recv_f.at[z], (r, 2 * z_peer(k) + h))
        left_cotangents()
        for k in range(1, Z):
            await_recv("f", rows(core, mine * Z + z_peer(k), piece), recv_f.at[z_peer(k)])
    else:
        left_cotangents()
    for k in range(1, R):
        push("d", rows(core, mine, blk), rows(core, mine, blk), recv_d.at[r], (row_peer(k), c))
    stage_2()
    push("e", rows(core, mine, blk), rows(core, mine, blk), recv_e.at[r], sib)

    for k in range(1, Z):
        src = 2 * z_peer(k) + h
        await_recv("u", rows(ug, src, um), recv_u.at[0, src])
        push("w", rows(ug, src, um), rows(ug, src, um), recv_u.at[0, src], sib)
    for k in range(1, R):
        q = row_peer(k)
        await_recv("d", rows(core, h * R + q, blk), recv_d.at[q])
        push("e", rows(core, h * R + q, blk), rows(core, h * R + q, blk), recv_e.at[q], sib)
    for k in range(Z):
        src = 2 * z_peer(k) + 1 - h
        await_recv("w", rows(ug, src, um), recv_u.at[0, src])
    uh[...], ul[...] = split(ug[...])
    xh[...], xl[...] = split(ug[...] * inv_row)
    for k in range(1, Z):
        src = 2 * z_peer(k) + h
        await_recv("u", rows(ucg, src, um), recv_u.at[1, src])
        push("w", rows(ucg, src, um), rows(ucg, src, um), recv_u.at[1, src], sib)
    width = 2 * LANES
    for q in range(R):
        await_recv("e", rows(core, (1 - h) * R + q, blk), recv_e.at[q])
    wh[...], wl[...] = split(core[...])
    for k in range(Z):
        src = 2 * z_peer(k) + 1 - h
        await_recv("w", rows(ucg, src, um), recv_u.at[1, src])

    @pl.loop(0, K // width)
    def _(i):
        here = pl.ds(pl.multiple_of(i * width, width), width)
        panel = dot3(uh[...], ul[...], wh[:, here], wl[:, here], NN)
        panel = panel + ucg[:, here] * (1.0 / s_ref[:, here])
        lh[:, here], ll[:, here] = split(panel)

    for k in range(1, n):
        await_recv("v", rows(vcg, a * n + b_peer(k), vm), recv_v.at[1, a * n + b_peer(k)])
        for j in range(1, n):
            src = a_peer(j) * n + b_peer(k)
            await_recv("v", rows(vcg, src, vm), recv_v.at[1, src])

    @pl.loop(0, out_ref.shape[1] // width)
    def _(i):
        here = pl.ds(pl.multiple_of(i * width, width), width)
        bh, bl = split(vcg[here, :])
        out_ref[:, here] = dot3(xh[...], xl[...], bh, bl, NT)

    for k in range(1, n):
        await_recv("v", rows(vg, a_peer(k) * n + b, vm), recv_v.at[0, a_peer(k) * n + b])
        for j in range(1, n):
            src = a_peer(k) * n + b_peer(j)
            await_recv("v", rows(vg, src, vm), recv_v.at[0, src])

    @pl.loop(0, out_ref.shape[1] // width)
    def _(i):
        here = pl.ds(pl.multiple_of(i * width, width), width)
        bh, bl = split(vg[here, :])
        out_ref[:, here] += dot3(lh[...], ll[...], bh, bl, NT)

    for copy in sends:
        copy.wait_send()


def local(R, C, left_factor, left_cotangent, right_factor, right_cotangent, singular, singular_cotangent):
    um, K = left_factor.shape
    vm = right_factor.shape[0]
    n, Z = math.isqrt(R), C // 2
    M, N = um * C, vm * R
    blk = K // 2 // R
    piece = blk // Z if blk % (8 * Z) == 0 else blk
    vmem = pl.BlockSpec(memory_space=pltpu.VMEM)
    dma = pltpu.SemaphoreType.DMA
    f32 = [
        (M, K), (M, K), (N, K), (N, K), (K, K), (K, K), (K, LANES), (K, K),
        (K // 2, K), (K // 2, K), (R * blk, K), (blk, K), (Z * piece, K), (K, K),
    ]
    b16 = [(K, K)] * 2 + [(M, K)] * 6
    scratch = [pltpu.VMEM(shape, F32) for shape in f32] + [pltpu.VMEM(shape, BF16) for shape in b16]
    scratch += [
        dma((4,)), dma((4 * (n - 1) + 2 * (n - 1) ** 2 + 4 * Z + 3 * R + 2 * Z,)),
        dma((2, R)), dma((2, C)), dma((1,)), dma((R,)), dma((Z,)), dma((R,)), dma((R,)), dma((Z,)),
    ]
    return pl.pallas_call(
        functools.partial(kernel, R, C),
        out_shape=jax.ShapeDtypeStruct((M, N), F32),
        in_specs=[pl.BlockSpec(memory_space=pltpu.HBM)] * 4 + [vmem] * 2,
        out_specs=vmem,
        scratch_shapes=scratch,
        compiler_params=pltpu.CompilerParams(
            collective_id=0, has_side_effects=True, vmem_limit_bytes=62 * 1024 * 1024
        ),
    )(
        left_factor, left_cotangent, right_factor, right_cotangent,
        singular.reshape(1, K), singular_cotangent.reshape(1, K),
    )


def solution(mesh):
    placed = (
        P(("row", "col"), None),
        P(("row", "col"), None),
        P(("col", "row"), None),
        P(("col", "row"), None),
        P(),
        P(),
    )
    return jax.shard_map(
        functools.partial(local, mesh.shape["row"], mesh.shape["col"]),
        mesh=mesh, in_specs=placed, out_specs=P("row", "col"), check_vma=False,
    )
```

time: 58.4 us -> 53 us (0.908)
  local copies, waits for them, and re-layouts: 6.31 us -> 2.65 us
  Pallas kernels: 51.6 us -> 50.1 us
    unnamed x13 -> x1, local copies, waits for them, and re-layouts: 6.31 us -> 2.65 us
    pallas_call x1, Pallas kernels: 51.6 us -> 50.1 us  [local(): pl.pallas_call(functools.partial(kernel, R, C), out_shape=jax.ShapeDtypeS...]
where the time goes in v2:
time: 53 us; the launch traced here: 52.8 us
  Pallas kernels  50.1 us (95%)
  local copies, waits for them, and re-layouts  2.65 us (5%)
    pallas_call x1, Pallas kernels, local(): pl.pallas_call(functools.partial(kernel, R, C), out_shape=jax.ShapeDtypeS...  50.1 us
    unnamed x1, local copies, waits for them, and re-layouts  2.65 us

profile of v2, /device:TPU:0, one launch (start us, length us, event | category | flops | bytes accessed | tf_op | source)
XLA Modules:
  0.0 52.8 jit_solution(2758062092233622083)
XLA Ops:
  0.0 50.1 %shard_map.64 = f32[512,768]{1,0:T(8,128)} custom-call(f32[64,512]{1,0:T(8,128)} %u_ref.1, f32[64,512]{1,0:T(8,128)} %uc_ref.1, f32[192,512]{1,0:T(8,128)} %v_ref.1, f32[192,512]{1,0:T(8,128)} %vc_ref.1, f32[1,512]{1,0:T(1,128)} %bitcast.2, f32[1,512]{1,0:T(1,128)} %bitcast.3), custom_call_target="tpu_custom_call" | custom-call | tf_op jit(solution)/shard_map/pallas_call | solution.py:278
  50.1 2.7 %copy.8 = f32[512,768]{1,0:T(8,128)} copy(f32[512,768]{1,0:T(8,128)} %shard_map.64) | data formatting | bytes 3145728

commit v3 on v2

--- a/solution.py
+++ b/solution.py
@@ -29,7 +29,8 @@
 
 def kernel(
     R, C,
-    u_ref, uc_ref, v_ref, vc_ref, s_ref, sc_ref, out_ref,
+    u_ref, uc_ref, v_ref, vc_ref, s_in, sc_in, out_ref,
+    s_ref, sc_ref,
     ug, ucg, vg, vcg, gl, gr, scol, part, ra, p1, rb, p2, rc, core,
     wh, wl, uh, ul, lh, ll, xh, xl,
     load, send, recv_v, recv_u, recv_a, recv_b, recv_c, recv_d, recv_e, recv_f,
@@ -65,18 +66,18 @@
         pltpu.make_async_copy(src, dst, load.at[i])
         for i, (src, dst) in enumerate((
             (u_ref, rows(ug, c, um)), (uc_ref, rows(ucg, c, um)),
-            (v_ref, rows(vg, r, vm)), (vc_ref, rows(vcg, r, vm)),
+            (v_ref, rows(vg, r, vm)), (vc_ref, rows(vcg, r, vm)), (s_in, s_ref), (sc_in, sc_ref),
         ))
     ]
+    barrier = pltpu.get_barrier_semaphore()
+    pl.semaphore_signal(barrier, inc=1, device_id=sib, device_id_type=MESH)
+    for k in range(1, R):
+        pl.semaphore_signal(barrier, inc=1, device_id=(row_peer(k), c), device_id_type=MESH)
+    for k in range(1, Z):
+        pl.semaphore_signal(barrier, inc=1, device_id=(r, 2 * z_peer(k) + h), device_id_type=MESH)
     for copy in loads:
         copy.start()
 
-    barrier = pltpu.get_barrier_semaphore()
-    pl.semaphore_signal(barrier, inc=1, device_id=sib, device_id_type=MESH)
-    for k in range(1, R):
-        pl.semaphore_signal(barrier, inc=1, device_id=(row_peer(k), c), device_id_type=MESH)
-    for k in range(1, Z):
-        pl.semaphore_signal(barrier, inc=1, device_id=(r, 2 * z_peer(k) + h), device_id_type=MESH)
     pl.semaphore_wait(barrier, 1 + (R - 1) + (Z - 1))
 
     sends = []
@@ -136,10 +137,6 @@
     for k in range(1, R):
         push("b", rows(p1, row_peer(k), blk), rows(rb, r, blk), recv_b.at[r], (row_peer(k), c))
     rows(rb, r, blk)[...] = rows(p1, r, blk)[...]
-    for k in range(1, n):
-        push("v", v_ref, rows(vg, r, vm), recv_v.at[0, r], (a_peer(k) * n + b, c))
-    for k in range(1, n):
-        push("v", vc_ref, rows(vcg, r, vm), recv_v.at[1, r], (a * n + b_peer(k), c))
     push("w", u_ref, rows(ug, c, um), recv_u.at[0, c], sib)
     push("w", uc_ref, rows(ucg, c, um), recv_u.at[1, c], sib)
     for k in range(1, R):
@@ -174,6 +171,10 @@
         rows(rc, z, blk)[...] = total
         for k in range(1, Z):
             push("c", rows(rc, z, blk), rows(rc, z, blk), recv_c.at[z], (r, 2 * z_peer(k) + h))
+    for k in range(1, n):
+        push("v", v_ref, rows(vg, r, vm), recv_v.at[0, r], (a_peer(k) * n + b, c))
+    for k in range(1, n):
+        push("v", vc_ref, rows(vcg, r, vm), recv_v.at[1, r], (a * n + b_peer(k), c))
     for k in range(1, Z):
         await_recv("c", rows(rc, z_peer(k), piece), recv_c.at[z_peer(k)])
     total = rc[0:piece, :]
@@ -186,9 +187,9 @@
     if piece != blk:
         for k in range(1, Z):
             push("f", rows(core, at, piece), rows(core, at, piece), recv_f.at[z], (r, 2 * z_peer(k) + h))
+        for k in range(1, Z):
+            await_recv("f", rows(core, mine * Z + z_peer(k), piece), recv_f.at[z_peer(k)])
         left_cotangents()
-        for k in range(1, Z):
-            await_recv("f", rows(core, mine * Z + z_peer(k), piece), recv_f.at[z_peer(k)])
     else:
         left_cotangents()
     for k in range(1, R):
@@ -228,29 +229,24 @@
         panel = panel + ucg[:, here] * (1.0 / s_ref[:, here])
         lh[:, here], ll[:, here] = split(panel)
 
+    def columns(q):
+        at = slice(q * vm, (q + 1) * vm)
+        bh, bl = split(vcg[at, :])
+        ch, cl = split(vg[at, :])
+        out_ref[:, at] = dot3(xh[...], xl[...], bh, bl, NT) + dot3(lh[...], ll[...], ch, cl, NT)
+
     for k in range(1, n):
         await_recv("v", rows(vcg, a * n + b_peer(k), vm), recv_v.at[1, a * n + b_peer(k)])
-        for j in range(1, n):
-            src = a_peer(j) * n + b_peer(k)
-            await_recv("v", rows(vcg, src, vm), recv_v.at[1, src])
-
-    @pl.loop(0, out_ref.shape[1] // width)
-    def _(i):
-        here = pl.ds(pl.multiple_of(i * width, width), width)
-        bh, bl = split(vcg[here, :])
-        out_ref[:, here] = dot3(xh[...], xl[...], bh, bl, NT)
-
-    for k in range(1, n):
         await_recv("v", rows(vg, a_peer(k) * n + b, vm), recv_v.at[0, a_peer(k) * n + b])
+    for q in range(R):
+        pl.when((a == q // n) | (b == q % n))(functools.partial(columns, q))
+    for k in range(1, n):
         for j in range(1, n):
             src = a_peer(k) * n + b_peer(j)
+            await_recv("v", rows(vcg, src, vm), recv_v.at[1, src])
             await_recv("v", rows(vg, src, vm), recv_v.at[0, src])
-
-    @pl.loop(0, out_ref.shape[1] // width)
-    def _(i):
-        here = pl.ds(pl.multiple_of(i * width, width), width)
-        bh, bl = split(vg[here, :])
-        out_ref[:, here] += dot3(lh[...], ll[...], bh, bl, NT)
+    for q in range(R):
+        pl.when((a != q // n) & (b != q % n))(functools.partial(columns, q))
 
     for copy in sends:
         copy.wait_send()
@@ -266,19 +262,20 @@
     vmem = pl.BlockSpec(memory_space=pltpu.VMEM)
     dma = pltpu.SemaphoreType.DMA
     f32 = [
+        (1, K), (1, K),
         (M, K), (M, K), (N, K), (N, K), (K, K), (K, K), (K, LANES), (K, K),
         (K // 2, K), (K // 2, K), (R * blk, K), (blk, K), (Z * piece, K), (K, K),
     ]
     b16 = [(K, K)] * 2 + [(M, K)] * 6
     scratch = [pltpu.VMEM(shape, F32) for shape in f32] + [pltpu.VMEM(shape, BF16) for shape in b16]
     scratch += [
-        dma((4,)), dma((4 * (n - 1) + 2 * (n - 1) ** 2 + 4 * Z + 3 * R + 2 * Z,)),
+        dma((6,)), dma((4 * (n - 1) + 2 * (n - 1) ** 2 + 4 * Z + 3 * R + 2 * Z,)),
         dma((2, R)), dma((2, C)), dma((1,)), dma((R,)), dma((Z,)), dma((R,)), dma((R,)), dma((Z,)),
     ]
     return pl.pallas_call(
         functools.partial(kernel, R, C),
         out_shape=jax.ShapeDtypeStruct((M, N), F32),
-        in_specs=[pl.BlockSpec(memory_space=pltpu.HBM)] * 4 + [vmem] * 2,
+        in_specs=[pl.BlockSpec(memory_space=pltpu.HBM)] * 6,
         out_specs=vmem,
         scratch_shapes=scratch,
         compiler_params=pltpu.CompilerParams(

time: 53 us -> 51.2 us (0.966)
  Pallas kernels: 50.1 us -> 48.4 us
    pallas_call x1, Pallas kernels: 50.1 us -> 48.4 us  [local(): pl.pallas_call(functools.partial(kernel, R, C), out_shape=jax.ShapeDtypeS...]
where the time goes in v3:
time: 51.2 us; the launch traced here: 51 us
  Pallas kernels  48.4 us (95%)
  local copies, waits for them, and re-layouts  2.65 us (5%)
    pallas_call x1, Pallas kernels, local(): pl.pallas_call(functools.partial(kernel, R, C), out_shape=jax.ShapeDtypeS...  48.4 us
    unnamed x1, local copies, waits for them, and re-layouts  2.65 us

profile of v3, /device:TPU:0, one launch (start us, length us, event | category | flops | bytes accessed | tf_op | source)
XLA Modules:
  0.0 51.0 jit_solution(4193334182777710992)
XLA Ops:
  0.0 48.4 %shard_map.64 = f32[512,768]{1,0:T(8,128)} custom-call(f32[64,512]{1,0:T(8,128)} %u_ref.1, f32[64,512]{1,0:T(8,128)} %uc_ref.1, f32[192,512]{1,0:T(8,128)} %v_ref.1, f32[192,512]{1,0:T(8,128)} %vc_ref.1, f32[1,512]{1,0:T(1,128)} %bitcast.2, f32[1,512]{1,0:T(1,128)} %bitcast.3), custom_call_target="tpu_custom_call" | custom-call | tf_op jit(solution)/shard_map/pallas_call | solution.py:275
  48.4 2.7 %copy.8 = f32[512,768]{1,0:T(8,128)} copy(f32[512,768]{1,0:T(8,128)} %shard_map.64) | data formatting | bytes 3145728
